TPU v7x, 512 devices: a whole 4x4x16 slice. The times are simulated.
512 devices in a mesh: gx: 8 (over y, z_hi), gy: 8 (over z_lo), gz: 8 (over x, core).
Axes of the slice: x: 4, y: 4, z: 16 (z_hi: 2, z_lo: 8; z = z_hi * 8 + z_lo), core: 2. Of those that a mesh axis runs over, the one named last changes fastest.
Arguments:
- attn_values: bfloat16 [3072, 4096], P('gy', ('gx', 'gz')), may hold values from -4 to 4
- attn_exponents: int32 [3072, 32], P('gy', 'gx'), may hold values from -4 to 0
- hidden_values: bfloat16 [3072, 14336], P('gy', ('gx', 'gz')), may hold values from -4 to 4
- hidden_exponents: int32 [3072, 112], P('gy', 'gx'), may hold values from -4 to 0
- attn_out_grad: bfloat16 [3072, 4096], P('gy', 'gz'), may hold values from -6 to 6
- mlp_out_grad: bfloat16 [3072, 4096], P('gy', 'gz'), may hold values from -6 to 6
- attn_weight: bfloat16 [4096, 4096], P(('gx', 'gy'), 'gz'), may hold values from -0.09375 to 0.09375
- mlp_weight: bfloat16 [14336, 4096], P(('gx', 'gy'), 'gz'), may hold values from -0.046875 to 0.046875
Outputs:
- attn_input_grad: bfloat16 [3072, 4096], P('gy', ('gx', 'gz'))
- mlp_input_grad: bfloat16 [3072, 14336], P('gy', ('gx', 'gz'))
- attn_weight_grad: bfloat16 [4096, 4096], P(('gx', 'gy'), 'gz')
- mlp_weight_grad: bfloat16 [14336, 4096], P(('gx', 'gy'), 'gz')
All inputs are finite; a program needn't handle non-finite values.
Results may differ from a plain program's by a relative error of at most 0.017.
Values may be sent and summed in bfloat16 or wider, within the bound.
A program may use at most 64 MiB of HBM per device.

v0:
```python
import jax
import jax.numpy as jnp
from jax import lax
from jax.sharding import PartitionSpec as P

BLOCK = 128


def dequantize(values, exponents):
    row_count, col_count = values.shape
    scales = jnp.exp2(exponents.astype(jnp.float32))
    widened = (
        values.astype(jnp.float32).reshape(row_count, col_count // BLOCK, BLOCK)
        * scales[:, :, None]
    )
    return widened.reshape(row_count, col_count).astype(jnp.bfloat16)


def contract_cols(left, right):
    return lax.dot_general(
        left, right, (((1,), (1,)), ((), ())), preferred_element_type=jnp.float32
    )


def blocked_sum(inputs_all, grads_all, groups):
    shaped_in = inputs_all.reshape(groups, -1, inputs_all.shape[1])
    shaped_grad = grads_all.reshape(groups, -1, grads_all.shape[1])
    partial_value = jnp.einsum(
        "gtk,gtn->gkn", shaped_in, shaped_grad, preferred_element_type=jnp.float32
    )
    kept = lax.optimization_barrier(partial_value.astype(jnp.bfloat16))
    return jnp.sum(kept.astype(jnp.float32), axis=0)


def on_device(
    attn_values,
    attn_exponents,
    hidden_values,
    hidden_exponents,
    attn_out_grad,
    mlp_out_grad,
    attn_weight,
    mlp_weight,
):
    attn_vals, hidden_vals = (
        lax.all_gather(attn_values, "gz", axis=1, tiled=True),
        lax.all_gather(hidden_values, "gz", axis=1, tiled=True),
    )
    attn_inputs = dequantize(attn_vals, attn_exponents)
    hidden_inputs = dequantize(hidden_vals, hidden_exponents)
    rows_attn, rows_mlp = (
        lax.all_gather(attn_weight, "gy", axis=0, tiled=True),
        lax.all_gather(mlp_weight, "gy", axis=0, tiled=True),
    )
    token_rows = attn_out_grad.shape[0]
    term_attn = contract_cols(attn_out_grad, rows_attn)
    term_mlp = contract_cols(mlp_out_grad, rows_mlp)
    summed_attn, summed_mlp = (
        lax.psum_scatter(
            term_attn.astype(jnp.bfloat16), "gz", scatter_dimension=1, tiled=True
        ).astype(jnp.float32),
        lax.psum_scatter(
            term_mlp.astype(jnp.bfloat16), "gz", scatter_dimension=1, tiled=True
        ).astype(jnp.float32),
    )
    attn_input_grad = summed_attn.astype(jnp.bfloat16)
    mlp_input_grad = summed_mlp.astype(jnp.bfloat16)
    groups = lax.axis_size("gy")
    sub_attn = attn_inputs.shape[1] // groups
    factor = float(token_rows * groups) ** (-0.5)
    all_attn, all_mlp = (
        lax.all_to_all(attn_inputs, "gy", split_axis=1, concat_axis=0, tiled=True),
        lax.all_to_all(hidden_inputs, "gy", split_axis=1, concat_axis=0, tiled=True),
    )
    all_grad_attn, all_grad_mlp = (
        lax.all_gather(attn_out_grad, "gy", axis=0, tiled=True),
        lax.all_gather(mlp_out_grad, "gy", axis=0, tiled=True),
    )
    summed = jnp.concatenate(
        [blocked_sum(all_attn, all_grad_attn, groups), blocked_sum(all_mlp, all_grad_mlp, groups)],
        axis=0,
    )
    scaled = (summed * factor).astype(jnp.bfloat16)
    attn_weight_grad = scaled[:sub_attn]
    mlp_weight_grad = scaled[sub_attn:]
    return (attn_input_grad, mlp_input_grad, attn_weight_grad, mlp_weight_grad)


def solution(mesh):
    placed = (
        P("gy", ("gx", "gz")),
        P("gy", "gx"),
        P("gy", ("gx", "gz")),
        P("gy", "gx"),
        P("gy", "gz"),
        P("gy", "gz"),
        P(("gx", "gy"), "gz"),
        P(("gx", "gy"), "gz"),
    )
    return jax.shard_map(
        on_device,
        mesh=mesh,
        in_specs=placed,
        out_specs=(
            P("gy", ("gx", "gz")),
            P("gy", ("gx", "gz")),
            P(("gx", "gy"), "gz"),
            P(("gx", "gy"), "gz"),
        ),
        check_vma=False,
    )
```

profile of v0, /device:TPU:1, one launch (start us, length us, event | category | flops | bytes accessed | tf_op | source)
XLA Modules:
  0.0 415.5 jit_solution(1901101355430849345)
XLA Ops:
  7.2 0.0 copy-start.3
  7.2 0.0 all-gather.9.cloned.1.call-start
  7.2 0.7 all-gather.9.cloned.1.call-update
  7.9 0.0 all-gather.5.cloned.1.call-start
  8.0 0.7 all-gather.5.cloned.1.call-update
  8.7 0.0 all-gather.7.cloned.1.call-start
  8.7 0.7 all-gather.7.cloned.1.call-update
  9.4 0.0 all-gather.11.cloned.1.call-start
  9.4 0.5 all-gather.11.cloned.1.call-update
  10.0 19.9 %all_gather.20 = bf16[384,512]{0,1:T(8,128)(2,1)S(1)} all-gather(bf16[384,64]{0,1:T(8,128)(2,1)} %param.8), channel_id=1, replica_groups=mesh['gx'=8,'gy'=8,'gz'=8] {'gz'}, dimensions={1}, use_global_device_ids=true | all-gather | bytes 442368 | tf_op jit(solution)/shard_map/all_gather | solution.py:46
  29.9 0.7 multiply_exponential_fusion.1
  30.6 0.9 fusion.2
  31.4 7.2 %all-to-all-start = ((bf16[384,8,64]{0,2,1:T(8,128)(2,1)}), bf16[384,8,64]{0,2,1:T(8,128)(2,1)S(1)}, u32[]{:S(2)}, u32[]{:S(2)}) async-start(bf16[384,8,64]{0,2,1:T(8,128)(2,1)} %bitcast.1), calls=%async_computation.2 | async-start | bytes 786432 | tf_op jit(solution)/shard_map/all_to_all | solution.py:72
  38.6 0.0 copy-done.3
  38.7 8.9 %all-gather.9.cloned.1.call-done = bf16[384,1792]{0,1:T(8,128)(2,1)} async-done(((bf16[384,224]{0,1:T(8,128)(2,1)}), bf16[384,1792]{0,1:T(8,128)(2,1)}) %all-gather.9.cloned.1.call-update) | async-done | bytes 1376272 | tf_op jit(solution)/shard_map/all_gather | solution.py:47
  47.5 2.8 fusion
  50.3 0.0 copy-start.2
  50.3 0.0 copy-start
  50.3 6.3 %all-to-all-done = bf16[384,8,64]{0,2,1:T(8,128)(2,1)S(1)} async-done(((bf16[384,8,64]{0,2,1:T(8,128)(2,1)}), bf16[384,8,64]{0,2,1:T(8,128)(2,1)S(1)}, u32[]{:S(2)}, u32[]{:S(2)}) %all-to-all-start) | async-done | bytes 393248 | tf_op jit(solution)/shard_map/all_to_all | solution.py:72
  56.6 9.4 %all-to-all-start.1 = ((bf16[384,8,224]{0,2,1:T(8,128)(2,1)}), bf16[384,8,224]{0,2,1:T(8,128)(2,1)S(1)}, u32[]{:S(2)}, u32[]{:S(2)}) async-start(bf16[384,8,224]{0,2,1:T(8,128)(2,1)} %bitcast.5), calls=%async_computation.3 | async-start | bytes 2752512 | tf_op jit(solution)/shard_map/all_to_all | solution.py:73
  66.0 0.0 copy-start.1
  66.0 0.0 reduce-scatter.3.cloned.1.call-start
  66.1 0.0 copy-done.2
  66.1 119.5 %all_gather.18 = bf16[512,512]{1,0:T(8,128)(2,1)S(1)} all-gather(bf16[64,512]{1,0:T(8,128)(2,1)S(1)} %copy-done.2), channel_id=1, replica_groups=mesh['gx'=8,'gy'=8,'gz'=8] {'gy'}, dimensions={0}, use_global_device_ids=true | all-gather | bytes 589824 | tf_op jit(solution)/shard_map/all_gather | solution.py:52
  185.6 0.0 copy-done
  185.6 1.2 convolution_convert_fusion.3
  186.8 0.0 reduce-scatter.3.cloned.1.call-update
  186.8 0.0 reduce-scatter.5.cloned.1.call-start
  186.9 0.0 all-gather.5.cloned.1.call-done
  186.9 0.0 copy-done.1
  186.9 3.8 convolution_convert_fusion
  190.7 0.0 reduce-scatter.5.cloned.1.call-update
  190.7 59.6 %all-gather.7.cloned.1.call-done = bf16[3072,512]{1,0:T(8,128)(2,1)} async-done(((bf16[384,512]{1,0:T(8,128)(2,1)}), bf16[3072,512]{1,0:T(8,128)(2,1)}) %all-gather.7.cloned.1.call-update) | async-done | bytes 3145744 | tf_op jit(solution)/shard_map/all_gather | solution.py:76
  250.3 2.6 convolution_convert_fusion.2
  252.9 0.1 convert_reduce_fusion.1
  252.9 78.3 %all-gather.11.cloned.1.call-done = bf16[3072,512]{1,0:T(8,128)(2,1)} async-done(((bf16[384,512]{1,0:T(8,128)(2,1)}), bf16[3072,512]{1,0:T(8,128)(2,1)}) %all-gather.11.cloned.1.call-update) | async-done | bytes 3145744 | tf_op jit(solution)/shard_map/all_gather | solution.py:77
  331.3 0.0 all-to-all-done.1
  331.3 3.0 convolution_convert_fusion.1
  334.3 0.3 convert_reduce_fusion
  334.6 0.7 slice.9
  335.3 0.6 slice.8
  335.9 30.4 %reduce-scatter.3.cloned.1.call-done = bf16[384,64]{0,1:T(8,128)(2,1)} async-done(((bf16[384,512]{0,1:T(8,128)(2,1)}), bf16[384,64]{0,1:T(8,128)(2,1)}) %reduce-scatter.3.cloned.1.call-update) | async-done | bytes 49168 | tf_op jit(solution)/shard_map/reduce_scatter | solution.py:59
  366.3 42.3 %reduce-scatter.5.cloned.1.call-done = bf16[384,224]{0,1:T(8,128)(2,1)} async-done(((bf16[384,1792]{0,1:T(8,128)(2,1)}), bf16[384,224]{0,1:T(8,128)(2,1)}) %reduce-scatter.5.cloned.1.call-update) | async-done | bytes 172048 | tf_op jit(solution)/shard_map/reduce_scatter | solution.py:62
  (2 shorter events, 0.1 us)
Async XLA Ops:
  7.2 31.5 %copy-start.3 = (s32[384,14]{0,1:T(8,128)S(1)}, s32[384,14]{0,1:T(8,128)}, u32[]{:S(2)}) copy-start(s32[384,14]{0,1:T(8,128)} %param.11) | copy-start | bytes 64516
  7.2 40.4 %all-gather.9.cloned.1.call-start = ((), (), s32[]{:S(2)}) async-start(), calls=%async_computation.8 | async-start | bytes 1548288 | tf_op jit(solution)/shard_map/all_gather | solution.py:47
  7.9 179.0 %all-gather.5.cloned.1.call-start = ((), (), s32[]{:S(2)}) async-start(), calls=%async_computation.5 | async-start | bytes 2064384 | tf_op jit(solution)/shard_map/all_gather | solution.py:53
  8.7 241.6 %all-gather.7.cloned.1.call-start = ((), (), s32[]{:S(2)}) async-start(), calls=%async_computation.7 | async-start | bytes 3538944 | tf_op jit(solution)/shard_map/all_gather | solution.py:76
  9.4 321.9 %all-gather.11.cloned.1.call-start = ((), (), s32[]{:S(2)}) async-start(), calls=%async_computation.9 | async-start | bytes 3538944 | tf_op jit(solution)/shard_map/all_gather | solution.py:77
  31.4 25.2 %all-to-all-start = ((bf16[384,8,64]{0,2,1:T(8,128)(2,1)}), bf16[384,8,64]{0,2,1:T(8,128)(2,1)S(1)}, u32[]{:S(2)}, u32[]{:S(2)}) async-start(bf16[384,8,64]{0,2,1:T(8,128)(2,1)} %bitcast.1), calls=%async_computation.2 | async-start | bytes 786432 | tf_op jit(solution)/shard_map/all_to_all | solution.py:72
  50.3 15.8 %copy-start.2 = (bf16[64,512]{1,0:T(8,128)(2,1)S(1)}, bf16[64,512]{1,0:T(8,128)(2,1)}, u32[]{:S(2)}) copy-start(bf16[64,512]{1,0:T(8,128)(2,1)} %param.14) | copy-start | bytes 196612
  50.3 135.3 %copy-start = (bf16[384,512]{1,0:T(8,128)(2,1)S(1)}, bf16[384,512]{1,0:T(8,128)(2,1)}, u32[]{:S(2)}) copy-start(bf16[384,512]{1,0:T(8,128)(2,1)} %param.12) | copy-start | bytes 1179652
  56.6 274.6 %all-to-all-start.1 = ((bf16[384,8,224]{0,2,1:T(8,128)(2,1)}), bf16[384,8,224]{0,2,1:T(8,128)(2,1)S(1)}, u32[]{:S(2)}, u32[]{:S(2)}) async-start(bf16[384,8,224]{0,2,1:T(8,128)(2,1)} %bitcast.5), calls=%async_computation.3 | async-start | bytes 2752512 | tf_op jit(solution)/shard_map/all_to_all | solution.py:73
  66.0 120.9 %copy-start.1 = (bf16[384,512]{1,0:T(8,128)(2,1)S(1)}, bf16[384,512]{1,0:T(8,128)(2,1)}, u32[]{:S(2)}) copy-start(bf16[384,512]{1,0:T(8,128)(2,1)} %param.13) | copy-start | bytes 1179652
  66.0 300.3 %reduce-scatter.3.cloned.1.call-start = ((), (), s32[]{:S(2)}) async-start(), calls=%async_computation.4 | async-start | bytes 442368 | tf_op jit(solution)/shard_map/reduce_scatter | solution.py:59
  186.8 221.8 %reduce-scatter.5.cloned.1.call-start = ((), (), s32[]{:S(2)}) async-start(), calls=%async_computation.6 | async-start | bytes 1548288 | tf_op jit(solution)/shard_map/reduce_scatter | solution.py:62
Sparse Core Ops, SparseCore 0:
  10.1 37.3 all-gather.8
  49.6 109.9 all-gather.4
  161.7 88.4 all-gather.6
  252.2 79.0 all-gather.10
  334.5 31.8 reduce-scatter.2
  369.8 38.7 reduce-scatter.4
where the time goes:
time: 417 us; the launch traced here: 416 us
  waiting for transfers between devices  228 us (55%)
  blocking collectives  139 us (33%)
  starting transfers between devices  16.9 us (4%)
  between operations  14.2 us (3%)
  matrix products  10.6 us (3%)
  other arithmetic  4.72 us (1%)
    all_gather x1, blocking collectives, on_device(): lax.all_gather(attn_weight, 'gy', axis=0, tiled=True)  119 us
    all_gather x1, waiting for transfers between devices, on_device(): lax.all_gather(mlp_out_grad, 'gy', axis=0, tiled=True)  78.3 us
    all_gather x1, waiting for transfers between devices, on_device(): lax.all_gather(attn_out_grad, 'gy', axis=0, tiled=True)  59.6 us
    reduce_scatter x1, waiting for transfers between devices, on_device(): lax.psum_scatter(term_mlp.astype(jnp.bfloat16), 'gz', scatter_dimension=1...  42.3 us
    reduce_scatter x1, waiting for transfers between devices, on_device(): lax.psum_scatter(term_attn.astype(jnp.bfloat16), 'gz', scatter_dimension=...  30.4 us
    all_gather x1, blocking collectives, on_device(): lax.all_gather(attn_values, 'gz', axis=1, tiled=True)  19.9 us
    all_to_all x1, starting transfers between devices, on_device(): lax.all_to_all(hidden_inputs, 'gy', split_axis=1, concat_axis=0, tiled=True)  9.42 us
    all_gather x1, waiting for transfers between devices, on_device(): lax.all_gather(hidden_values, 'gz', axis=1, tiled=True)  8.87 us
  transfers between devices with their start and end apart: 8, of which 6 were waited for; matrix products, arithmetic and copies ran while one was open for 4% of the time, Pallas kernels for 0%

commit v1 on v0

v1 whole, which is shorter than its diff:
```python
import functools

import jax
import jax.numpy as jnp
from jax import lax
from jax.experimental import pallas as pl
from jax.experimental.pallas import tpu as pltpu
from jax.sharding import PartitionSpec as P

BLOCK = 128
N = 8
NX = 4
CHUNKS = 3
MESH = pl.DeviceIdType.MESH
F32 = jnp.float32
BF16 = jnp.bfloat16


def dequantize(values, exponents):
    tokens, width = values.shape
    scales = jnp.exp2(exponents.astype(F32))
    wide = jnp.repeat(scales, BLOCK, axis=1)
    mine = lax.dynamic_slice_in_dim(wide, lax.axis_index("gz") * width, width, axis=1)
    return (values.astype(F32) * mine).astype(BF16)


def kernel(
    factor, xt, ga, gm, wa, wm, dxt, dwa, dwm,
    wown, xf, ru, rd, p, qk, qs, qc, qp, qr, dxa,
    us, ur, ds, dr, xs, xr, cs, cr, qcs, qcr, qxs, qxr,
):
    gx, k, gz = lax.axis_index("gx"), lax.axis_index("gy"), lax.axis_index("gz")
    x, c = gz // 2, gz % 2
    sib = (gx, k, 2 * x + 1 - c)
    rows_a = wa.shape[0]
    rows = rows_a + wm.shape[0]
    step = rows // CHUNKS
    above, below = (gx, k + 1, gz), (gx, k - 1, gz)

    def chip(other):
        return (gx, k, 2 * other + c)

    barrier = pltpu.get_barrier_semaphore()

    def greet(device):
        pl.semaphore_signal(barrier, inc=1, device_id=device, device_id_type=MESH)

    greet(sib)
    for d in (1, 2, 3):
        greet(chip((x + d) % NX))
    pl.when(k < N - 1)(lambda: greet(above))
    pl.when(k > 0)(lambda: greet(below))
    pl.semaphore_wait(barrier, NX + (k < N - 1).astype(jnp.int32) + (k > 0).astype(jnp.int32))

    def remote(src, dst, send, recv, device):
        return pltpu.make_async_remote_copy(
            src_ref=src, dst_ref=dst, send_sem=send, recv_sem=recv, device_id=device, device_id_type=MESH
        )

    wown[:rows_a] = wa[...]
    wown[rows_a:] = wm[...]

    def up(s, i, src):
        at = pl.ds(i * step, step)
        index = (k - s + N) % N
        source = wown.at[at] if src is None else ru.at[index, at]
        return remote(source, ru.at[index, at], us.at[s, i], ur.at[s, i], above)

    def down(s, i, src):
        at = pl.ds(i * step, step)
        index = (k + s) % N
        source = wown.at[at] if src is None else rd.at[index, at]
        return remote(source, rd.at[index, at], ds.at[s, i], dr.at[s, i], below)

    for i in range(CHUNKS):
        pl.when(k < N - 1)(lambda: up(0, i, None).start())
        pl.when(k > 0)(lambda: down(0, i, None).start())

    def x_copy(d):
        return remote(xt, xf.at[gz], xs.at[d], xr.at[d], chip((x + d) % NX))

    def core_copy(d):
        index = 2 * ((x - d + NX) % NX) + c
        return remote(xt if d == 0 else xf.at[index], xf.at[index], cs.at[d], cr.at[d], sib)

    for d in (1, 3, 2):
        x_copy(d).start()
    core_copy(0).start()

    def grad_dot(w, j):
        dims = (((1,), (1,)), ((), ()))
        top = lax.dot_general(w[:rows_a], ga[...], dims, preferred_element_type=F32)
        low = lax.dot_general(w[rows_a:], gm[...], dims, preferred_element_type=F32)
        xj, cj = j // 2, j % 2
        qk[xj, :rows_a] = top
        qk[xj, rows_a:] = low

        @pl.when(cj != c)
        def _():
            qs[xj] = qk[xj].astype(BF16)
            remote(qs.at[xj], qc.at[xj], qcs.at[xj], qcr.at[xj], sib).start()

    def pair_sum(j):
        xj, cj = j // 2, j % 2

        @pl.when(cj == c)
        def _():
            remote(qs.at[xj], qc.at[xj], qcs.at[xj], qcr.at[xj], sib).wait_recv()

            @pl.when(xj != x)
            def _():
                qp[xj] = (qk[xj] + qc[xj].astype(F32)).astype(BF16)
                remote(qp.at[xj], qr.at[x], qxs.at[xj], qxr.at[x], chip(xj)).start()

            @pl.when(xj == x)
            def _():
                dxa[...] = qk[xj] + qc[xj].astype(F32)

    def weight_dot(source, index):
        p[index, :rows_a] = jnp.dot(source[:rows_a], ga[...], preferred_element_type=F32)
        p[index, rows_a:] = jnp.dot(source[rows_a:], gm[...], preferred_element_type=F32)

    grad_dot(wown, k)
    weight_dot(xt, gz)

    def slot(s, kinds):
        for i in range(CHUNKS):
            at = pl.ds(i * step, step)
            for buf, copy, first, last, index, weights in (
                (ru, up, k == 0, k == N - 1, (k - s + N) % N, s <= k),
                (rd, down, k == N - 1, k == 0, (k + s) % N, s <= N - 1 - k),
            ):
                if "w" in kinds:
                    @pl.when(weights)
                    def _():
                        copy(s - 1, i, 1).wait_recv()

                        @pl.when(jnp.logical_not(last))
                        def _():
                            copy(s, i, 1).start()

                if "s" in kinds:
                    @pl.when(jnp.logical_not(weights | last))
                    def _():
                        @pl.when(jnp.logical_not(first))
                        def _():
                            copy(s - 1, i, 1).wait_recv()
                            buf[index, at] = (p[index, at] + buf[index, at].astype(F32)).astype(BF16)

                        @pl.when(first)
                        def _():
                            buf[index, at] = p[index, at].astype(BF16)

                        copy(s, i, 1).start()

    def input_parts(s):
        @pl.when(k - s >= 0)
        def _():
            grad_dot(ru.at[k - s], k - s)

        @pl.when(k + s < N)
        def _():
            grad_dot(rd.at[k + s], k + s)

    def input_sums(s):
        pl.when(k - s >= 0)(lambda: pair_sum(k - s))
        pl.when(k + s < N)(lambda: pair_sum(k + s))

    slot(1, "w")
    for d in (1, 3, 2):
        x_copy(d).wait_recv()
        core_copy(d).start()
        index = 2 * ((x - d + NX) % NX) + c
        weight_dot(xf.at[index], index)
    for d in (0, 1, 3, 2):
        core_copy(d).wait_recv()
        index = 2 * ((x - d + NX) % NX) + 1 - c
        weight_dot(xf.at[index], index)
    slot(1, "s")
    pair_sum(k)
    input_parts(1)

    def body(s, carry):
        slot(s, "ws")
        input_sums(s - 1)
        input_parts(s)
        return carry

    lax.fori_loop(2, N, body, 0)
    input_sums(N - 1)

    for buf, copy, none in ((ru, up, k == 0), (rd, down, k == N - 1)):
        @pl.when(jnp.logical_not(none))
        def _():
            for i in range(CHUNKS):
                copy(N - 1, i, 1).wait_recv()
            p[k] = p[k] + buf[k].astype(F32)

    dwa[...] = (p[k, :rows_a] * factor).astype(BF16)
    dwm[...] = (p[k, rows_a:] * factor).astype(BF16)

    for d in (1, 3, 2):
        other = (x - d + NX) % NX
        remote(qp.at[other], qr.at[other], qxs.at[other], qxr.at[other], chip(other)).wait_recv()
        dxa[...] = dxa[...] + qr[other].astype(F32)
    dxt[...] = dxa[...].astype(BF16)

    for d in (1, 2, 3):
        x_copy(d).wait_send()
        other = (x + d) % NX
        remote(qp.at[other], qr.at[other], qxs.at[other], qxr.at[other], chip(other)).wait_send()
    for d in range(NX):
        core_copy(d).wait_send()
        remote(qs.at[d], qc.at[d], qcs.at[d], qcr.at[d], sib).wait_send()

    def sent(s, carry):
        for i in range(CHUNKS):
            pl.when(k < N - 1)(lambda: up(s, i, 1).wait_send())
            pl.when(k > 0)(lambda: down(s, i, 1).wait_send())
        return carry

    lax.fori_loop(0, N, sent, 0)


def on_device(
    attn_values,
    attn_exponents,
    hidden_values,
    hidden_exponents,
    attn_out_grad,
    mlp_out_grad,
    attn_weight,
    mlp_weight,
):
    tokens, width = attn_out_grad.shape
    rows_a, rows_m = attn_weight.shape[0], mlp_weight.shape[0]
    rows = rows_a + rows_m
    inputs = jnp.concatenate(
        [dequantize(attn_values, attn_exponents), dequantize(hidden_values, hidden_exponents)], axis=1
    ).T
    factor = float(tokens * N) ** (-0.5)
    vmem = pl.BlockSpec(memory_space=pltpu.VMEM)
    dma = pltpu.SemaphoreType.DMA
    dxt, dwa, dwm = pl.pallas_call(
        functools.partial(kernel, factor),
        out_shape=(
            jax.ShapeDtypeStruct((rows, tokens), BF16),
            jax.ShapeDtypeStruct((rows_a, width), BF16),
            jax.ShapeDtypeStruct((rows_m, width), BF16),
        ),
        in_specs=[vmem] * 5,
        out_specs=[vmem] * 3,
        scratch_shapes=[
            pltpu.VMEM((rows, width), BF16),
            pltpu.VMEM((N, rows, tokens), BF16),
            pltpu.VMEM((N, rows, width), BF16),
            pltpu.VMEM((N, rows, width), BF16),
            pltpu.VMEM((N, rows, width), F32),
            pltpu.VMEM((NX, rows, tokens), F32),
            pltpu.VMEM((NX, rows, tokens), BF16),
            pltpu.VMEM((NX, rows, tokens), BF16),
            pltpu.VMEM((NX, rows, tokens), BF16),
            pltpu.VMEM((NX, rows, tokens), BF16),
            pltpu.VMEM((rows, tokens), F32),
            dma((N, CHUNKS)),
            dma((N, CHUNKS)),
            dma((N, CHUNKS)),
            dma((N, CHUNKS)),
            dma((NX,)),
            dma((NX,)),
            dma((NX,)),
            dma((NX,)),
            dma((NX,)),
            dma((NX,)),
            dma((NX,)),
            dma((NX,)),
        ],
        compiler_params=pltpu.CompilerParams(
            collective_id=0, has_side_effects=True, vmem_limit_bytes=40 * 2**20
        ),
    )(inputs, attn_out_grad, mlp_out_grad, attn_weight, mlp_weight)
    grads = dxt.T
    return (grads[:, :rows_a], grads[:, rows_a:], dwa, dwm)


def solution(mesh):
    placed = (
        P("gy", ("gx", "gz")),
        P("gy", "gx"),
        P("gy", ("gx", "gz")),
        P("gy", "gx"),
        P("gy", "gz"),
        P("gy", "gz"),
        P(("gx", "gy"), "gz"),
        P(("gx", "gy"), "gz"),
    )
    return jax.shard_map(
        on_device,
        mesh=mesh,
        in_specs=placed,
        out_specs=(
            P("gy", ("gx", "gz")),
            P("gy", ("gx", "gz")),
            P(("gx", "gy"), "gz"),
            P(("gx", "gy"), "gz"),
        ),
        check_vma=False,
    )
```

time: 417 us -> 74 us (0.18)
  waiting for transfers between devices: 228 us -> 0 us
  blocking collectives: 139 us -> 0 us
  Pallas kernels: 0 us -> 69.2 us
  starting transfers between devices: 16.9 us -> 0 us
  between operations: 14.2 us -> 0.8 us
  matrix products: 10.6 us -> 0 us
    all_gather x4 -> x0, waiting for transfers between devices: 147 us -> none  [the longest x1 78.3 us: on_device(): lax.all_gather(mlp_out_grad, 'gy', axis=0, tiled=True)]
    all_gather x2 -> x0, blocking collectives: 139 us -> none  [the longest x1 119 us: on_device(): lax.all_gather(attn_weight, 'gy', axis=0, tiled=True)]
    reduce_scatter x2 -> x0, waiting for transfers between devices: 72.8 us -> none  [the longest x1 42.3 us: on_device(): lax.psum_scatter(term_mlp.astype(jnp.bfloat16), 'gz', scatter_dimension=1...]
    pallas_call x0 -> x1, Pallas kernels: none -> 69.2 us  [on_device(): pl.pallas_call(functools.partial(kernel, factor), out_shape=(jax.ShapeDty...]
    all_to_all x2 -> x0, starting transfers between devices: 16.6 us -> none  [the longest x1 9.42 us: on_device(): lax.all_to_all(hidden_inputs, 'gy', split_axis=1, concat_axis=0, tiled=True)]
    dot_general x4 -> x0, matrix products: 10.6 us -> none  [the longest x2 5.57 us: blocked_sum(): jnp.einsum('gtk,gtn->gkn', shaped_in, shaped_grad, preferred_element_type...]
    all_to_all x2 -> x0, waiting for transfers between devices: 6.29 us -> none  [the longest x1 6.29 us: on_device(): lax.all_to_all(attn_inputs, 'gy', split_axis=1, concat_axis=0, tiled=True)]
  transfers between devices with their start and end apart: 8 -> 0, of which waited for: 6 -> 0; matrix products, arithmetic and copies ran while one was open for 4% -> 0% of each run, Pallas kernels for 0% -> 0%
where the time goes in v1:
time: 74 us; the launch traced here: 73.9 us
  Pallas kernels  69.2 us (94%)
  local copies, waits for them, and re-layouts  2.9 us (4%)
  other arithmetic  0.94 us (1%)
  between operations  0.8 us (1%)
    pallas_call x1, Pallas kernels, on_device(): pl.pallas_call(functools.partial(kernel, factor), out_shape=(jax.ShapeDty...  69.2 us

profile of v1, /device:TPU:1, one launch (start us, length us, event | category | flops | bytes accessed | tf_op | source)
XLA Modules:
  0.0 73.9 jit_solution(2812255902341997831)
XLA Ops:
  0.6 0.0 copy-start.4
  0.6 0.0 copy-start.6
  0.7 0.0 copy-start.5
  0.7 0.0 copy-start
  0.7 0.0 copy-start.1
  0.7 0.0 copy-start.3
  0.7 0.0 copy-start.2
  0.7 0.8 %multiply_exponential_fusion = f32[384,14]{0,1:T(8,128)S(1)} fusion(s32[384,14]{0,1:T(8,128)} %param.11), kind=kLoop, calls=%fused_computation.3 | loop fusion | flops 10752 | bytes 43008 | tf_op jit(solution)/shard_map/exp2 | solution.py:21
  1.6 0.2 broadcast_in_dim.7
  1.7 0.0 copy-done.4
  1.8 0.0 copy-done.6
  1.8 0.1 broadcast_in_dim.6
  1.9 0.0 copy-done.5
  2.0 0.0 copy-done
  2.0 0.0 copy-done.1
  2.0 0.0 copy-done.3
  2.0 0.0 copy-done.2
  2.0 69.2 %shard_map.111 = (bf16[288,384]{1,0:T(8,128)(2,1)S(1)}, bf16[64,512]{1,0:T(8,128)(2,1)S(1)}, bf16[224,512]{1,0:T(8,128)(2,1)S(1)}) custom-call(bf16[288,384]{1,0:T(8,128)(2,1)S(1)} %maximum_bitcast_fusion.xt, bf16[384,512]{1,0:T(8,128)(2,1)S(1)} %copy-done, bf16[384,512]{1,0:T(8,128)(2,1)S(1)} %copy-done.1, bf16[64,512]{1,0:T(8,128)(2,1)S(1)} %copy-done.3, ...), custom_call_target="tpu_custom_call" | custom-call | tf_op jit(solution)/shard_map/pallas_call | solution.py:244
  71.2 0.7 slice.9
  71.9 0.6 slice.8
  72.5 0.6 copy.14
  73.2 0.7 copy.15
  (4 shorter events, 0.1 us)
Async XLA Ops:
  0.6 1.1 %copy-start.4 = (bf16[384,224]{0,1:T(8,128)(2,1)S(1)}, bf16[384,224]{0,1:T(8,128)(2,1)}, u32[]{:S(2)}) copy-start(bf16[384,224]{0,1:T(8,128)(2,1)} %param.10) | copy-start | bytes 516100
  0.6 1.2 %copy-start.6 = (s32[384,4]{0,1:T(4,128)S(1)}, s32[384,4]{0,1:T(4,128)}, u32[]{:S(2)}) copy-start(s32[384,4]{0,1:T(4,128)} %param.9) | copy-start | bytes 18436
  0.7 1.2 %copy-start.5 = (bf16[384,64]{0,1:T(8,128)(2,1)S(1)}, bf16[384,64]{0,1:T(8,128)(2,1)}, u32[]{:S(2)}) copy-start(bf16[384,64]{0,1:T(8,128)(2,1)} %param.8) | copy-start | bytes 147460
  0.7 1.3 %copy-start = (bf16[384,512]{1,0:T(8,128)(2,1)S(1)}, bf16[384,512]{1,0:T(8,128)(2,1)}, u32[]{:S(2)}) copy-start(bf16[384,512]{1,0:T(8,128)(2,1)} %ga.1) | copy-start | bytes 1179652
  0.7 1.3 %copy-start.1 = (bf16[384,512]{1,0:T(8,128)(2,1)S(1)}, bf16[384,512]{1,0:T(8,128)(2,1)}, u32[]{:S(2)}) copy-start(bf16[384,512]{1,0:T(8,128)(2,1)} %gm.1) | copy-start | bytes 1179652
  0.7 1.3 %copy-start.3 = (bf16[64,512]{1,0:T(8,128)(2,1)S(1)}, bf16[64,512]{1,0:T(8,128)(2,1)}, u32[]{:S(2)}) copy-start(bf16[64,512]{1,0:T(8,128)(2,1)} %wa.1) | copy-start | bytes 196612
  0.7 1.3 %copy-start.2 = (bf16[224,512]{1,0:T(8,128)(2,1)S(1)}, bf16[224,512]{1,0:T(8,128)(2,1)}, u32[]{:S(2)}) copy-start(bf16[224,512]{1,0:T(8,128)(2,1)} %wm.1) | copy-start | bytes 688132

commit v2 on v1

v2 whole, which is shorter than its diff:
```python
import functools

import jax
import jax.numpy as jnp
from jax import lax
from jax.experimental import pallas as pl
from jax.experimental.pallas import tpu as pltpu
from jax.sharding import PartitionSpec as P

BLOCK = 128
N = 8
NX = 4
CHUNKS = 6
PIECES = 3
MESH = pl.DeviceIdType.MESH
F32 = jnp.float32
BF16 = jnp.bfloat16


def when(condition, *actions):
    @pl.when(condition)
    def _():
        for action in actions:
            action()


def kernel(
    factor, xa_in, xm_in, ea_in, em_in, ga_in, gm_in, wa_in, wm_in, dxa, dxm, dwa, dwm,
    xa, xm, ea, em, ga, gm, w, xt, xf, ru, rd, p, qk, qs, qc, qp, qr, total,
    ins, us, ur, ds, dr, xs, xr, cs, cr, qcs, qcr, qxs, qxr,
):
    gx, k, gz = lax.axis_index("gx"), lax.axis_index("gy"), lax.axis_index("gz")
    x, c = gz // 2, gz % 2
    sib = (gx, k, 2 * x + 1 - c)
    rows_a, rows_m = wa_in.shape[0], wm_in.shape[0]
    rows = rows_a + rows_m
    step = rows // CHUNKS
    piece = rows // PIECES
    above, below = (gx, k + 1, gz), (gx, k - 1, gz)

    def chip(other):
        return (gx, k, 2 * other + c)

    barrier = pltpu.get_barrier_semaphore()

    def greet(device):
        pl.semaphore_signal(barrier, inc=1, device_id=device, device_id_type=MESH)

    greet(sib)
    for d in (1, 2, 3):
        greet(chip((x + d) % NX))
    when(k < N - 1, lambda: greet(above))
    when(k > 0, lambda: greet(below))

    loads = [
        pltpu.make_async_copy(src, dst, ins.at[i])
        for i, (src, dst) in enumerate(
            (
                (xa_in, xa), (ea_in, ea), (xm_in, xm), (em_in, em),
                (wa_in, w.at[pl.ds(0, rows_a)]), (wm_in, w.at[pl.ds(rows_a, rows_m)]), (ga_in, ga), (gm_in, gm),
            )
        )
    ]
    for load in loads:
        load.start()
    for load in loads[:4]:
        load.wait()

    def scaled(values, exponents, at, size, first):
        row = (gz * values.shape[0] + at) // BLOCK
        scale = jnp.exp2(exponents[pl.ds(row, 1), :].astype(F32))
        xt[first + at : first + at + size] = (values[at : at + size].astype(F32) * scale).astype(BF16)

    unit = 32
    for at in range(0, rows_a, unit):
        scaled(xa, ea, at, unit, 0)
    for at in range(0, rows_m, unit):
        scaled(xm, em, at, unit, rows_a)
    for load in loads[4:]:
        load.wait()
    pl.semaphore_wait(barrier, NX + (k < N - 1).astype(jnp.int32) + (k > 0).astype(jnp.int32))

    def remote(src, dst, send, recv, device):
        return pltpu.make_async_remote_copy(
            src_ref=src, dst_ref=dst, send_sem=send, recv_sem=recv, device_id=device, device_id_type=MESH
        )

    def up(s, i, own=False):
        at = pl.ds(i * step, step)
        index = (k - s + N) % N
        return remote(w.at[at] if own else ru.at[index, at], ru.at[index, at], us.at[s, i], ur.at[s, i], above)

    def down(s, i, own=False):
        at = pl.ds(i * step, step)
        index = (k + s) % N
        return remote(w.at[at] if own else rd.at[index, at], rd.at[index, at], ds.at[s, i], dr.at[s, i], below)

    def x_copy(d, h):
        at = pl.ds(h * piece, piece)
        return remote(xt.at[at], xf.at[gz, at], xs.at[d, h], xr.at[d, h], chip((x + d) % NX))

    def core_copy(d, h):
        at = pl.ds(h * piece, piece)
        index = 2 * ((x - d + NX) % NX) + c
        source = xt.at[at] if d == 0 else xf.at[index, at]
        return remote(source, xf.at[index, at], cs.at[d, h], cr.at[d, h], sib)

    for i in range(CHUNKS):
        when(k < N - 1, lambda: up(0, i, True).start())
        when(k > 0, lambda: down(0, i, True).start())
        if i < PIECES:
            for d in (1, 3, 2):
                x_copy(d, i).start()
            core_copy(0, i).start()
    xf[gz] = xt[...]

    def grad_dot(source, j):
        dims = (((1,), (1,)), ((), ()))
        top = lax.dot_general(source[:rows_a], ga[...], dims, preferred_element_type=F32)
        low = lax.dot_general(source[rows_a:], gm[...], dims, preferred_element_type=F32)
        xj, cj = j // 2, j % 2
        qk[xj, :rows_a] = top
        qk[xj, rows_a:] = low

        @pl.when(cj != c)
        def _():
            qs[xj] = qk[xj].astype(BF16)
            remote(qs.at[xj], qc.at[xj], qcs.at[xj], qcr.at[xj], sib).start()

    def pair_sum(j):
        xj, cj = j // 2, j % 2

        @pl.when(cj == c)
        def _():
            remote(qs.at[xj], qc.at[xj], qcs.at[xj], qcr.at[xj], sib).wait_recv()

            @pl.when(xj != x)
            def _():
                qp[xj] = (qk[xj] + qc[xj].astype(F32)).astype(BF16)
                remote(qp.at[xj], qr.at[x], qxs.at[xj], qxr.at[x], chip(xj)).start()

            @pl.when(xj == x)
            def _():
                total[...] = qk[xj] + qc[xj].astype(F32)

    def weight_dot(index, lo, hi):
        if lo < rows_a:
            p[index, lo:rows_a] = jnp.dot(xf[index, lo:rows_a], ga[...], preferred_element_type=F32)
            lo = rows_a
        p[index, lo:hi] = jnp.dot(xf[index, lo:hi], gm[...], preferred_element_type=F32)

    def sides(s):
        return (
            (ru, up, k == 0, k == N - 1, (k - s + N) % N, s <= k),
            (rd, down, k == N - 1, k == 0, (k + s) % N, s <= N - 1 - k),
        )

    def forward(s, i, kinds="ws"):
        at = pl.ds(i * step, step)
        for buf, copy, first, last, index, weights in sides(s):
            if "w" in kinds:
                @pl.when(weights)
                def _():
                    copy(s - 1, i).wait_recv()
                    when(jnp.logical_not(last), lambda: copy(s, i).start())

            if "s" in kinds:
                @pl.when(jnp.logical_not(weights | last))
                def _():
                    @pl.when(jnp.logical_not(first))
                    def _():
                        copy(s - 1, i).wait_recv()
                        buf[index, at] = (p[index, at] + buf[index, at].astype(F32)).astype(BF16)

                    @pl.when(first)
                    def _():
                        buf[index, at] = p[index, at].astype(BF16)

                    copy(s, i).start()

    def input_part(s, side):
        j = k - s if side == 0 else k + s
        when((j >= 0) & (j < N), lambda: grad_dot((ru, rd)[side].at[j], j))

    def input_sums(s):
        for j in (k - s, k + s):
            when((j >= 0) & (j < N), lambda: pair_sum(j))

    def next_partial(s, side, lo=0, hi=rows):
        _, _, _, last, index, weights = sides(s)[side]
        when(jnp.logical_not(weights | last), lambda: weight_dot(index, lo, hi))

    def x_wait(h):
        for d in (1, 3, 2):
            x_copy(d, h).wait_recv()
            core_copy(d, h).start()

    def core_wait(h):
        for d in (0, 1, 3, 2):
            core_copy(d, h).wait_recv()
        for side in range(2):
            next_partial(1, side, h * piece, (h + 1) * piece)
        for i in range(h * CHUNKS // PIECES, (h + 1) * CHUNKS // PIECES):
            forward(1, i, "s")

    grad_dot(w, k)
    for i in range(3):
        forward(1, i, "w")
    x_wait(0)
    for i in range(3, 5):
        forward(1, i, "w")
    core_wait(0)
    forward(1, 5, "w")
    x_wait(1)
    core_wait(1)
    pair_sum(k)
    x_wait(2)
    core_wait(2)
    for side in range(2):
        next_partial(2, side)

    def body(s, carry):
        forward(s, 0)
        input_part(s - 1, 0)
        forward(s, 1)
        input_part(s - 1, 1)
        forward(s, 2)
        next_partial(s + 1, 0)
        forward(s, 3)
        next_partial(s + 1, 1)
        forward(s, 4)
        input_sums(s - 1)
        forward(s, 5)
        return carry

    lax.fori_loop(2, N, body, 0)
    for side in range(2):
        input_part(N - 1, side)
    weight_dot(k, 0, rows)
    input_sums(N - 1)
    for d in (1, 3, 2):
        other = (x - d + NX) % NX
        remote(qp.at[other], qr.at[other], qxs.at[other], qxr.at[other], chip(other)).wait_recv()
        total[...] = total[...] + qr[other].astype(F32)
    dxa[...] = total[:rows_a].astype(BF16)
    dxm[...] = total[rows_a:].astype(BF16)

    for i in range(CHUNKS):
        at = pl.ds(i * step, step)
        for buf, copy, none in ((ru, up, k == 0), (rd, down, k == N - 1)):
            @pl.when(jnp.logical_not(none))
            def _():
                copy(N - 1, i).wait_recv()
                p[k, at] = p[k, at] + buf[k, at].astype(F32)

    dwa[...] = (p[k, :rows_a] * factor).astype(BF16)
    dwm[...] = (p[k, rows_a:] * factor).astype(BF16)

    for d in (1, 2, 3):
        for h in range(PIECES):
            x_copy(d, h).wait_send()
        other = (x + d) % NX
        remote(qp.at[other], qr.at[other], qxs.at[other], qxr.at[other], chip(other)).wait_send()
    for d in range(NX):
        for h in range(PIECES):
            core_copy(d, h).wait_send()
        remote(qs.at[d], qc.at[d], qcs.at[d], qcr.at[d], sib).wait_send()

    def sent(s, carry):
        for i in range(CHUNKS):
            when(k < N - 1, lambda: up(s, i).wait_send())
            when(k > 0, lambda: down(s, i).wait_send())
        return carry

    lax.fori_loop(0, N, sent, 0)


def write_out(*refs):
    n = len(refs) // 2
    sems = refs[-1]
    copies = [pltpu.make_async_copy(refs[i], refs[n + i], sems.at[i]) for i in range(n)]
    for copy in copies:
        copy.start()
    for copy in copies:
        copy.wait()


def on_device(
    attn_values,
    attn_exponents,
    hidden_values,
    hidden_exponents,
    attn_out_grad,
    mlp_out_grad,
    attn_weight,
    mlp_weight,
):
    tokens, width = attn_out_grad.shape
    rows_a, rows_m = attn_weight.shape[0], mlp_weight.shape[0]
    rows = rows_a + rows_m
    factor = float(tokens * N) ** (-0.5)
    vmem = pl.BlockSpec(memory_space=pltpu.VMEM)
    hbm = pl.BlockSpec(memory_space=pl.ANY)
    dma = pltpu.SemaphoreType.DMA
    inputs = (
        attn_values.T,
        hidden_values.T,
        attn_exponents.T,
        hidden_exponents.T,
        attn_out_grad,
        mlp_out_grad,
        attn_weight,
        mlp_weight,
    )
    shapes = (
        jax.ShapeDtypeStruct((rows_a, tokens), BF16),
        jax.ShapeDtypeStruct((rows_m, tokens), BF16),
        jax.ShapeDtypeStruct((rows_a, width), BF16),
        jax.ShapeDtypeStruct((rows_m, width), BF16),
    )
    results = pl.pallas_call(
        functools.partial(kernel, factor),
        out_shape=shapes,
        in_specs=[hbm] * 8,
        out_specs=[vmem] * 4,
        scratch_shapes=[
            *[pltpu.VMEM(a.shape, a.dtype) for a in inputs[:6]],
            pltpu.VMEM((rows, width), BF16),
            pltpu.VMEM((rows, tokens), BF16),
            pltpu.VMEM((N, rows, tokens), BF16),
            pltpu.VMEM((N, rows, width), BF16),
            pltpu.VMEM((N, rows, width), BF16),
            pltpu.VMEM((N, rows, width), F32),
            pltpu.VMEM((NX, rows, tokens), F32),
            *[pltpu.VMEM((NX, rows, tokens), BF16)] * 4,
            pltpu.VMEM((rows, tokens), F32),
            dma((8,)),
            *[dma((N, CHUNKS))] * 4,
            *[dma((NX, PIECES))] * 4,
            *[dma((NX,))] * 4,
        ],
        compiler_params=pltpu.CompilerParams(
            collective_id=0, has_side_effects=True, vmem_limit_bytes=56 * 2**20
        ),
    )(*inputs)
    dxa, dxm, dwa, dwm = pl.pallas_call(
        write_out,
        out_shape=shapes,
        in_specs=[vmem] * 4,
        out_specs=[hbm] * 4,
        scratch_shapes=[dma((4,))],
    )(*results)
    return (dxa.T, dxm.T, dwa, dwm)


def solution(mesh):
    placed = (
        P("gy", ("gx", "gz")),
        P("gy", "gx"),
        P("gy", ("gx", "gz")),
        P("gy", "gx"),
        P("gy", "gz"),
        P("gy", "gz"),
        P(("gx", "gy"), "gz"),
        P(("gx", "gy"), "gz"),
    )
    return jax.shard_map(
        on_device,
        mesh=mesh,
        in_specs=placed,
        out_specs=(
            P("gy", ("gx", "gz")),
            P("gy", ("gx", "gz")),
            P(("gx", "gy"), "gz"),
            P(("gx", "gy"), "gz"),
        ),
        check_vma=False,
    )
```

time: 74 us -> 68.6 us (0.927)
  local copies, waits for them, and re-layouts: 2.9 us -> 0 us
  Pallas kernels: 69.2 us -> 67.6 us
  other arithmetic: 0.94 us -> 0 us
    pallas_call x1 -> x2, Pallas kernels: 69.2 us -> 67.6 us  [the longest x1 65.7 us: on_device(): pl.pallas_call(functools.partial(kernel, factor), out_shape=shapes, in_sp...]
    unnamed x16 -> x0, local copies, waits for them, and re-layouts: 1.35 us -> none
    slice x2 -> x0, local copies, waits for them, and re-layouts: 1.31 us -> none  [on_device(): return (grads[:, :rows_a], grads[:, rows_a:], dwa, dwm)]
    exp2 x2 -> x0, other arithmetic: 0.85 us -> none  [dequantize(): scales = jnp.exp2(exponents.astype(F32))]
where the time goes in v2:
time: 68.6 us; the launch traced here: 68.3 us
  Pallas kernels  67.6 us (99%)
    pallas_call x1, Pallas kernels, on_device(): pl.pallas_call(functools.partial(kernel, factor), out_shape=shapes, in_sp...  65.7 us
    pallas_call x1, Pallas kernels, on_device(): pl.pallas_call(write_out, out_shape=shapes, in_specs=[vmem] * 4, out_spec...  1.89 us

profile of v2, /device:TPU:1, one launch (start us, length us, event | category | flops | bytes accessed | tf_op | source)
XLA Modules:
  0.0 68.3 jit_solution(5172532065996684642)
XLA Ops:
  0.6 65.7 %shard_map.111 = (bf16[64,384]{1,0:T(8,128)(2,1)}, bf16[224,384]{1,0:T(8,128)(2,1)}, bf16[64,512]{1,0:T(8,128)(2,1)}, bf16[224,512]{1,0:T(8,128)(2,1)}) custom-call(bf16[64,384]{1,0:T(8,128)(2,1)} %bitcast.7, bf16[224,384]{1,0:T(8,128)(2,1)} %bitcast.6, s32[4,384]{1,0:T(4,128)} %bitcast.9, s32[14,384]{1,0:T(8,128)} %bitcast.8, bf16[384,512]{1,0:T(8,128)(2,1)} %ga_in.1, ...), custom_call_target="tpu_custom_call" | custom-call | tf_op jit(solution)/shard_map/pallas_call | solution.py:321
  66.4 1.9 %shard_map.112 = (bf16[64,384]{1,0:T(8,128)(2,1)}, bf16[224,384]{1,0:T(8,128)(2,1)}, bf16[64,512]{1,0:T(8,128)(2,1)}, bf16[224,512]{1,0:T(8,128)(2,1)}) custom-call(bf16[64,384]{1,0:T(8,128)(2,1)} %get-tuple-element.12.refs_0_, bf16[224,384]{1,0:T(8,128)(2,1)} %get-tuple-element.13.refs_1_, bf16[64,512]{1,0:T(8,128)(2,1)} %get-tuple-element.14.refs_2_, ...), custom_call_target="tpu_custom_call" | custom-call | tf_op jit(solution)/shard_map/pallas_call | solution.py:346

commit v3 on v2

--- a/solution.py
+++ b/solution.py
@@ -56,14 +56,52 @@
         pltpu.make_async_copy(src, dst, ins.at[i])
         for i, (src, dst) in enumerate(
             (
-                (xa_in, xa), (ea_in, ea), (xm_in, xm), (em_in, em),
-                (wa_in, w.at[pl.ds(0, rows_a)]), (wm_in, w.at[pl.ds(rows_a, rows_m)]), (ga_in, ga), (gm_in, gm),
+                (wa_in, w.at[pl.ds(0, rows_a)]), (wm_in, w.at[pl.ds(rows_a, rows_m)]),
+                (xa_in, xa), (ea_in, ea), (xm_in, xm), (em_in, em), (ga_in, ga), (gm_in, gm),
             )
         )
     ]
     for load in loads:
         load.start()
-    for load in loads[:4]:
+    for load in loads[:2]:
+        load.wait()
+    pl.semaphore_wait(barrier, NX + (k < N - 1).astype(jnp.int32) + (k > 0).astype(jnp.int32))
+
+    def remote(src, dst, send, recv, device):
+        return pltpu.make_async_remote_copy(
+            src_ref=src, dst_ref=dst, send_sem=send, recv_sem=recv, device_id=device, device_id_type=MESH
+        )
+
+    def up(s, i, own=False):
+        at = pl.ds(i * step, step)
+        index = (k - s + N) % N
+        return remote(w.at[at] if own else ru.at[index, at], ru.at[index, at], us.at[s, i], ur.at[s, i], above)
+
+    def down(s, i, own=False):
+        at = pl.ds(i * step, step)
+        index = (k + s) % N
+        return remote(w.at[at] if own else rd.at[index, at], rd.at[index, at], ds.at[s, i], dr.at[s, i], below)
+
+    def x_copy(d, h):
+        at = pl.ds(h * piece, piece)
+        return remote(xt.at[at], xf.at[gz, at], xs.at[d, h], xr.at[d, h], chip((x + d) % NX))
+
+    def core_copy(d, h):
+        at = pl.ds(h * piece, piece)
+        index = 2 * ((x - d + NX) % NX) + c
+        source = xt.at[at] if d == 0 else xf.at[index, at]
+        return remote(source, xf.at[index, at], cs.at[d, h], cr.at[d, h], sib)
+
+    def remote_pass(d, h):
+        at = pl.ds(h * piece, piece)
+        index = 2 * ((x - d + NX) % NX) + c
+        return remote(xf.at[index, at], xf.at[index, at], cs.at[d, h], cr.at[d, h], sib)
+
+    for i in range(CHUNKS):
+        when(k < N - 1, lambda: up(0, i, True).start())
+        when(k > 0, lambda: down(0, i, True).start())
+
+    for load in loads[2:6]:
         load.wait()
 
     def scaled(values, exponents, at, size, first):
@@ -76,72 +114,69 @@
         scaled(xa, ea, at, unit, 0)
     for at in range(0, rows_m, unit):
         scaled(xm, em, at, unit, rows_a)
-    for load in loads[4:]:
+
+    ahead = jnp.where(k < N // 2, NX - 1, 0)
+    held = ((k == 0) | (k == N - 1)) & (x != ahead)
+
+    def x_start():
+        for h in range(PIECES):
+            for d in (1, 3, 2):
+                x_copy(d, h).start()
+
+    when(jnp.logical_not(held), x_start)
+    for h in range(PIECES):
+        core_copy(0, h).start()
+    xf[gz] = xt[...]
+    for load in loads[6:]:
         load.wait()
-    pl.semaphore_wait(barrier, NX + (k < N - 1).astype(jnp.int32) + (k > 0).astype(jnp.int32))
-
-    def remote(src, dst, send, recv, device):
-        return pltpu.make_async_remote_copy(
-            src_ref=src, dst_ref=dst, send_sem=send, recv_sem=recv, device_id=device, device_id_type=MESH
-        )
-
-    def up(s, i, own=False):
-        at = pl.ds(i * step, step)
-        index = (k - s + N) % N
-        return remote(w.at[at] if own else ru.at[index, at], ru.at[index, at], us.at[s, i], ur.at[s, i], above)
-
-    def down(s, i, own=False):
-        at = pl.ds(i * step, step)
-        index = (k + s) % N
-        return remote(w.at[at] if own else rd.at[index, at], rd.at[index, at], ds.at[s, i], dr.at[s, i], below)
-
-    def x_copy(d, h):
+
+    def to_core(xj, h):
         at = pl.ds(h * piece, piece)
-        return remote(xt.at[at], xf.at[gz, at], xs.at[d, h], xr.at[d, h], chip((x + d) % NX))
-
-    def core_copy(d, h):
+        return remote(qs.at[xj, at], qc.at[xj, at], qcs.at[xj, h], qcr.at[xj, h], sib)
+
+    def to_chip(xj, h, sender):
         at = pl.ds(h * piece, piece)
-        index = 2 * ((x - d + NX) % NX) + c
-        source = xt.at[at] if d == 0 else xf.at[index, at]
-        return remote(source, xf.at[index, at], cs.at[d, h], cr.at[d, h], sib)
-
-    for i in range(CHUNKS):
-        when(k < N - 1, lambda: up(0, i, True).start())
-        when(k > 0, lambda: down(0, i, True).start())
-        if i < PIECES:
-            for d in (1, 3, 2):
-                x_copy(d, i).start()
-            core_copy(0, i).start()
-    xf[gz] = xt[...]
-
-    def grad_dot(source, j):
+        return remote(qp.at[xj, at], qr.at[sender, at], qxs.at[xj, h], qxr.at[sender, h], chip(xj))
+
+    def grad_dot(source, j, pieces=range(PIECES)):
         dims = (((1,), (1,)), ((), ()))
-        top = lax.dot_general(source[:rows_a], ga[...], dims, preferred_element_type=F32)
-        low = lax.dot_general(source[rows_a:], gm[...], dims, preferred_element_type=F32)
         xj, cj = j // 2, j % 2
-        qk[xj, :rows_a] = top
-        qk[xj, rows_a:] = low
+        lo, hi = pieces[0] * piece, (pieces[-1] + 1) * piece
+        cut = min(max(lo, rows_a), hi)
+        for first, end, grads in ((lo, cut, ga), (cut, hi, gm)):
+            if first < end:
+                part = lax.dot_general(source[first:end], grads[...], dims, preferred_element_type=F32)
+
+                @pl.when(cj == c)
+                def _():
+                    qk[xj, first:end] = part
+
+                @pl.when(cj != c)
+                def _():
+                    qs[xj, first:end] = part.astype(BF16)
 
         @pl.when(cj != c)
         def _():
-            qs[xj] = qk[xj].astype(BF16)
-            remote(qs.at[xj], qc.at[xj], qcs.at[xj], qcr.at[xj], sib).start()
-
-    def pair_sum(j):
+            for h in pieces:
+                to_core(xj, h).start()
+
+    def pair_sum(j, pieces=range(PIECES)):
         xj, cj = j // 2, j % 2
 
         @pl.when(cj == c)
         def _():
-            remote(qs.at[xj], qc.at[xj], qcs.at[xj], qcr.at[xj], sib).wait_recv()
-
-            @pl.when(xj != x)
-            def _():
-                qp[xj] = (qk[xj] + qc[xj].astype(F32)).astype(BF16)
-                remote(qp.at[xj], qr.at[x], qxs.at[xj], qxr.at[x], chip(xj)).start()
-
-            @pl.when(xj == x)
-            def _():
-                total[...] = qk[xj] + qc[xj].astype(F32)
+            for h in pieces:
+                lo, hi = h * piece, (h + 1) * piece
+                to_core(xj, h).wait_recv()
+
+                @pl.when(xj != x)
+                def _():
+                    qp[xj, lo:hi] = (qk[xj, lo:hi] + qc[xj, lo:hi].astype(F32)).astype(BF16)
+                    to_chip(xj, h, x).start()
+
+                @pl.when(xj == x)
+                def _():
+                    total[lo:hi] = qk[xj, lo:hi] + qc[xj, lo:hi].astype(F32)
 
     def weight_dot(index, lo, hi):
         if lo < rows_a:
@@ -178,101 +213,167 @@
 
                     copy(s, i).start()
 
-    def input_part(s, side):
+    def input_part(s, side, pieces=range(PIECES)):
         j = k - s if side == 0 else k + s
-        when((j >= 0) & (j < N), lambda: grad_dot((ru, rd)[side].at[j], j))
-
-    def input_sums(s):
+        when((j >= 0) & (j < N), lambda: grad_dot((ru, rd)[side].at[j], j, pieces))
+
+    def input_sums(s, pieces=range(PIECES)):
         for j in (k - s, k + s):
-            when((j >= 0) & (j < N), lambda: pair_sum(j))
+            when((j >= 0) & (j < N), lambda: pair_sum(j, pieces))
 
     def next_partial(s, side, lo=0, hi=rows):
         _, _, _, last, index, weights = sides(s)[side]
         when(jnp.logical_not(weights | last), lambda: weight_dot(index, lo, hi))
 
-    def x_wait(h):
-        for d in (1, 3, 2):
+    def x_wait(n, h):
+        d = (x - jnp.where(k < N // 2, NX - 1 - n, n) + NX) % NX
+
+        @pl.when(d != 0)
+        def _():
             x_copy(d, h).wait_recv()
-            core_copy(d, h).start()
-
-    def core_wait(h):
-        for d in (0, 1, 3, 2):
-            core_copy(d, h).wait_recv()
+            remote_pass(d, h).start()
+
+    def core_wait(n, h):
+        d = (x - jnp.where(k < N // 2, NX - 1 - n, n) + NX) % NX
+        remote_pass(d, h).wait_recv()
+
+    def first_sums(h):
         for side in range(2):
             next_partial(1, side, h * piece, (h + 1) * piece)
         for i in range(h * CHUNKS // PIECES, (h + 1) * CHUNKS // PIECES):
             forward(1, i, "s")
 
     grad_dot(w, k)
-    for i in range(3):
+    for i in range(2):
         forward(1, i, "w")
-    x_wait(0)
-    for i in range(3, 5):
-        forward(1, i, "w")
-    core_wait(0)
+    x_wait(0, 0)
+    when(held, x_start)
+    forward(1, 2, "w")
+    core_wait(0, 0)
+    first_sums(0)
+    forward(1, 3, "w")
+    x_wait(0, 1)
+    forward(1, 4, "w")
+    core_wait(0, 1)
+    first_sums(1)
     forward(1, 5, "w")
-    x_wait(1)
-    core_wait(1)
+    x_wait(0, 2)
     pair_sum(k)
-    x_wait(2)
-    core_wait(2)
+    core_wait(0, 2)
+    first_sums(2)
     for side in range(2):
         next_partial(2, side)
+
+    forward(2, 0)
+    for h in range(PIECES):
+        x_wait(1, h)
+    forward(2, 1)
+    for h in range(PIECES):
+        core_wait(1, h)
+    input_part(1, 0)
+    forward(2, 2)
+    for h in range(PIECES):
+        x_wait(2, h)
+    input_part(1, 1)
+    forward(2, 3)
+    for h in range(PIECES):
+        x_wait(3, h)
+    next_partial(3, 0)
+    forward(2, 4)
+    next_partial(3, 1)
+    forward(2, 5)
+    for n in (2, 3):
+        for h in range(PIECES):
+            core_wait(n, h)
+    input_sums(1)
+
+    def gone(s, i):
+        when(k < N - 1, lambda: up(s, i).wait_send())
+        when(k > 0, lambda: down(s, i).wait_send())
 
     def body(s, carry):
         forward(s, 0)
         input_part(s - 1, 0)
+        gone(s - 3, 0)
         forward(s, 1)
         input_part(s - 1, 1)
+        gone(s - 3, 1)
         forward(s, 2)
         next_partial(s + 1, 0)
+        gone(s - 3, 2)
         forward(s, 3)
         next_partial(s + 1, 1)
+        gone(s - 3, 3)
         forward(s, 4)
         input_sums(s - 1)
+        gone(s - 3, 4)
         forward(s, 5)
+        gone(s - 3, 5)
         return carry
 
-    lax.fori_loop(2, N, body, 0)
-    for side in range(2):
-        input_part(N - 1, side)
+    lax.fori_loop(3, N - 2, body, 0)
+
+    for s in (N - 2, N - 1):
+        for h in range(PIECES):
+            for i in range(h * CHUNKS // PIECES, (h + 1) * CHUNKS // PIECES):
+                forward(s, i)
+                gone(s - 3, i)
+            for side in range(2):
+                input_part(s, side, (h,))
+                if s == N - 2:
+                    next_partial(s + 1, side, h * piece, (h + 1) * piece)
+            if s == N - 2 and h < 2:
+                input_part(s - 1, h)
+            if h > 0:
+                input_sums(s, (h - 1,))
+        if s == N - 2:
+            input_sums(s - 1)
+        input_sums(s, (PIECES - 1,))
     weight_dot(k, 0, rows)
-    input_sums(N - 1)
-    for d in (1, 3, 2):
-        other = (x - d + NX) % NX
-        remote(qp.at[other], qr.at[other], qxs.at[other], qxr.at[other], chip(other)).wait_recv()
-        total[...] = total[...] + qr[other].astype(F32)
-    dxa[...] = total[:rows_a].astype(BF16)
-    dxm[...] = total[rows_a:].astype(BF16)
-
+    for d in (1, 2, 3):
+        for h in range(PIECES):
+            x_copy(d, h).wait_send()
+    for d in range(NX):
+        for h in range(PIECES):
+            core_copy(d, h).wait_send()
+    for s in (N - 3, N - 2):
+        for i in range(CHUNKS):
+            gone(s, i)
+
+    def last_sums():
+        for d in (1, 3, 2):
+            other = (x - d + NX) % NX
+            for h in range(PIECES):
+                to_chip(other, h, other).wait_recv()
+            total[...] = total[...] + qr[other].astype(F32)
+        dxa[...] = total[:rows_a].astype(BF16)
+        dxm[...] = total[rows_a:].astype(BF16)
+
+    def last_rows():
+        for i in range(CHUNKS):
+            lo, hi = i * step, (i + 1) * step
+            for buf, copy, none in ((ru, up, k == 0), (rd, down, k == N - 1)):
+                @pl.when(jnp.logical_not(none))
+                def _():
+                    copy(N - 1, i).wait_recv()
+                    p[k, lo:hi] = p[k, lo:hi] + buf[k, lo:hi].astype(F32)
+
+            cut = min(max(lo, rows_a), hi)
+            if lo < cut:
+                dwa[lo:cut] = (p[k, lo:cut] * factor).astype(BF16)
+            if cut < hi:
+                dwm[cut - rows_a : hi - rows_a] = (p[k, cut:hi] * factor).astype(BF16)
+
+    last_rows()
+    last_sums()
+    for d in (1, 2, 3):
+        for h in range(PIECES):
+            to_chip((x + d) % NX, h, x).wait_send()
+    for d in range(NX):
+        for h in range(PIECES):
+            to_core(d, h).wait_send()
     for i in range(CHUNKS):
-        at = pl.ds(i * step, step)
-        for buf, copy, none in ((ru, up, k == 0), (rd, down, k == N - 1)):
-            @pl.when(jnp.logical_not(none))
-            def _():
-                copy(N - 1, i).wait_recv()
-                p[k, at] = p[k, at] + buf[k, at].astype(F32)
-
-    dwa[...] = (p[k, :rows_a] * factor).astype(BF16)
-    dwm[...] = (p[k, rows_a:] * factor).astype(BF16)
-
-    for d in (1, 2, 3):
-        for h in range(PIECES):
-            x_copy(d, h).wait_send()
-        other = (x + d) % NX
-        remote(qp.at[other], qr.at[other], qxs.at[other], qxr.at[other], chip(other)).wait_send()
-    for d in range(NX):
-        for h in range(PIECES):
-            core_copy(d, h).wait_send()
-        remote(qs.at[d], qc.at[d], qcs.at[d], qcr.at[d], sib).wait_send()
-
-    def sent(s, carry):
-        for i in range(CHUNKS):
-            when(k < N - 1, lambda: up(s, i).wait_send())
-            when(k > 0, lambda: down(s, i).wait_send())
-        return carry
-
-    lax.fori_loop(0, N, sent, 0)
+        gone(N - 1, i)
 
 
 def write_out(*refs):
@@ -336,8 +437,7 @@
             pltpu.VMEM((rows, tokens), F32),
             dma((8,)),
             *[dma((N, CHUNKS))] * 4,
-            *[dma((NX, PIECES))] * 4,
-            *[dma((NX,))] * 4,
+            *[dma((NX, PIECES))] * 8,
         ],
         compiler_params=pltpu.CompilerParams(
             collective_id=0, has_side_effects=True, vmem_limit_bytes=56 * 2**20

time: 68.6 us -> 66.5 us (0.969)
  Pallas kernels: 67.6 us -> 65.7 us
    pallas_call x1, Pallas kernels: 65.7 us -> 63.8 us  [on_device(): pl.pallas_call(functools.partial(kernel, factor), out_shape=shapes, in_sp...]
where the time goes in v3:
time: 66.5 us; the launch traced here: 66.4 us
  Pallas kernels  65.7 us (99%)
    pallas_call x1, Pallas kernels, on_device(): pl.pallas_call(functools.partial(kernel, factor), out_shape=shapes, in_sp...  63.8 us
    pallas_call x1, Pallas kernels, on_device(): pl.pallas_call(write_out, out_shape=shapes, in_specs=[vmem] * 4, out_spec...  1.89 us

profile of v3, /device:TPU:1, one launch (start us, length us, event | category | flops | bytes accessed | tf_op | source)
XLA Modules:
  0.0 66.4 jit_solution(6758136850279582516)
XLA Ops:
  0.6 63.8 %shard_map.111 = (bf16[64,384]{1,0:T(8,128)(2,1)}, bf16[224,384]{1,0:T(8,128)(2,1)}, bf16[64,512]{1,0:T(8,128)(2,1)}, bf16[224,512]{1,0:T(8,128)(2,1)}) custom-call(bf16[64,384]{1,0:T(8,128)(2,1)} %bitcast.7, bf16[224,384]{1,0:T(8,128)(2,1)} %bitcast.6, s32[4,384]{1,0:T(4,128)} %bitcast.9, s32[14,384]{1,0:T(8,128)} %bitcast.8, bf16[384,512]{1,0:T(8,128)(2,1)} %ga_in.1, ...), custom_call_target="tpu_custom_call" | custom-call | tf_op jit(solution)/shard_map/pallas_call | solution.py:422
  64.5 1.9 %shard_map.112 = (bf16[64,384]{1,0:T(8,128)(2,1)}, bf16[224,384]{1,0:T(8,128)(2,1)}, bf16[64,512]{1,0:T(8,128)(2,1)}, bf16[224,512]{1,0:T(8,128)(2,1)}) custom-call(bf16[64,384]{1,0:T(8,128)(2,1)} %get-tuple-element.12.refs_0_, bf16[224,384]{1,0:T(8,128)(2,1)} %get-tuple-element.13.refs_1_, bf16[64,512]{1,0:T(8,128)(2,1)} %get-tuple-element.14.refs_2_, ...), custom_call_target="tpu_custom_call" | custom-call | tf_op jit(solution)/shard_map/pallas_call | solution.py:446

commit v4 on v3

--- a/solution.py
+++ b/solution.py
@@ -10,7 +10,7 @@
 BLOCK = 128
 N = 8
 NX = 4
-CHUNKS = 6
+CHUNKS = 3
 PIECES = 3
 MESH = pl.DeviceIdType.MESH
 F32 = jnp.float32
@@ -244,19 +244,16 @@
             forward(1, i, "s")
 
     grad_dot(w, k)
-    for i in range(2):
-        forward(1, i, "w")
+    forward(1, 0, "w")
     x_wait(0, 0)
     when(held, x_start)
-    forward(1, 2, "w")
     core_wait(0, 0)
     first_sums(0)
-    forward(1, 3, "w")
+    forward(1, 1, "w")
     x_wait(0, 1)
-    forward(1, 4, "w")
     core_wait(0, 1)
     first_sums(1)
-    forward(1, 5, "w")
+    forward(1, 2, "w")
     x_wait(0, 2)
     pair_sum(k)
     core_wait(0, 2)
@@ -267,21 +264,18 @@
     forward(2, 0)
     for h in range(PIECES):
         x_wait(1, h)
-    forward(2, 1)
     for h in range(PIECES):
         core_wait(1, h)
     input_part(1, 0)
-    forward(2, 2)
+    forward(2, 1)
     for h in range(PIECES):
         x_wait(2, h)
     input_part(1, 1)
-    forward(2, 3)
     for h in range(PIECES):
         x_wait(3, h)
     next_partial(3, 0)
-    forward(2, 4)
+    forward(2, 2)
     next_partial(3, 1)
-    forward(2, 5)
     for n in (2, 3):
         for h in range(PIECES):
             core_wait(n, h)
@@ -294,21 +288,15 @@
     def body(s, carry):
         forward(s, 0)
         input_part(s - 1, 0)
+        input_part(s - 1, 1)
         gone(s - 3, 0)
         forward(s, 1)
-        input_part(s - 1, 1)
+        next_partial(s + 1, 0)
+        next_partial(s + 1, 1)
         gone(s - 3, 1)
         forward(s, 2)
-        next_partial(s + 1, 0)
+        input_sums(s - 1)
         gone(s - 3, 2)
-        forward(s, 3)
-        next_partial(s + 1, 1)
-        gone(s - 3, 3)
-        forward(s, 4)
-        input_sums(s - 1)
-        gone(s - 3, 4)
-        forward(s, 5)
-        gone(s - 3, 5)
         return carry
 
     lax.fori_loop(3, N - 2, body, 0)

time: 66.5 us -> 65.7 us (0.988)
  Pallas kernels: 65.7 us -> 64.9 us
    pallas_call x1, Pallas kernels: 63.8 us -> 63 us  [on_device(): pl.pallas_call(functools.partial(kernel, factor), out_shape=shapes, in_sp...]
where the time goes in v4:
time: 65.7 us; the launch traced here: 65.5 us
  Pallas kernels  64.9 us (99%)
    pallas_call x1, Pallas kernels, on_device(): pl.pallas_call(functools.partial(kernel, factor), out_shape=shapes, in_sp...  63 us
    pallas_call x1, Pallas kernels, on_device(): pl.pallas_call(write_out, out_shape=shapes, in_specs=[vmem] * 4, out_spec...  1.89 us

profile of v4, /device:TPU:1, one launch (start us, length us, event | category | flops | bytes accessed | tf_op | source)
XLA Modules:
  0.0 65.5 jit_solution(16591253726088624834)
XLA Ops:
  0.6 63.0 %shard_map.111 = (bf16[64,384]{1,0:T(8,128)(2,1)}, bf16[224,384]{1,0:T(8,128)(2,1)}, bf16[64,512]{1,0:T(8,128)(2,1)}, bf16[224,512]{1,0:T(8,128)(2,1)}) custom-call(bf16[64,384]{1,0:T(8,128)(2,1)} %bitcast.7, bf16[224,384]{1,0:T(8,128)(2,1)} %bitcast.6, s32[4,384]{1,0:T(4,128)} %bitcast.9, s32[14,384]{1,0:T(8,128)} %bitcast.8, bf16[384,512]{1,0:T(8,128)(2,1)} %ga_in.1, ...), custom_call_target="tpu_custom_call" | custom-call | tf_op jit(solution)/shard_map/pallas_call | solution.py:410
  63.6 1.9 %shard_map.112 = (bf16[64,384]{1,0:T(8,128)(2,1)}, bf16[224,384]{1,0:T(8,128)(2,1)}, bf16[64,512]{1,0:T(8,128)(2,1)}, bf16[224,512]{1,0:T(8,128)(2,1)}) custom-call(bf16[64,384]{1,0:T(8,128)(2,1)} %get-tuple-element.12.refs_0_, bf16[224,384]{1,0:T(8,128)(2,1)} %get-tuple-element.13.refs_1_, bf16[64,512]{1,0:T(8,128)(2,1)} %get-tuple-element.14.refs_2_, ...), custom_call_target="tpu_custom_call" | custom-call | tf_op jit(solution)/shard_map/pallas_call | solution.py:434

commit v5 on v4

--- a/solution.py
+++ b/solution.py
@@ -56,15 +56,13 @@
         pltpu.make_async_copy(src, dst, ins.at[i])
         for i, (src, dst) in enumerate(
             (
+                (xa_in, xa), (ea_in, ea), (xm_in, xm), (em_in, em), (ga_in, ga), (gm_in, gm),
                 (wa_in, w.at[pl.ds(0, rows_a)]), (wm_in, w.at[pl.ds(rows_a, rows_m)]),
-                (xa_in, xa), (ea_in, ea), (xm_in, xm), (em_in, em), (ga_in, ga), (gm_in, gm),
             )
         )
     ]
     for load in loads:
         load.start()
-    for load in loads[:2]:
-        load.wait()
     pl.semaphore_wait(barrier, NX + (k < N - 1).astype(jnp.int32) + (k > 0).astype(jnp.int32))
 
     def remote(src, dst, send, recv, device):
@@ -72,15 +70,15 @@
             src_ref=src, dst_ref=dst, send_sem=send, recv_sem=recv, device_id=device, device_id_type=MESH
         )
 
-    def up(s, i, own=False):
+    def up(s, i):
         at = pl.ds(i * step, step)
         index = (k - s + N) % N
-        return remote(w.at[at] if own else ru.at[index, at], ru.at[index, at], us.at[s, i], ur.at[s, i], above)
-
-    def down(s, i, own=False):
+        return remote(ru.at[index, at], ru.at[index, at], us.at[s, i], ur.at[s, i], above)
+
+    def down(s, i):
         at = pl.ds(i * step, step)
         index = (k + s) % N
-        return remote(w.at[at] if own else rd.at[index, at], rd.at[index, at], ds.at[s, i], dr.at[s, i], below)
+        return remote(rd.at[index, at], rd.at[index, at], ds.at[s, i], dr.at[s, i], below)
 
     def x_copy(d, h):
         at = pl.ds(h * piece, piece)
@@ -97,11 +95,21 @@
         index = 2 * ((x - d + NX) % NX) + c
         return remote(xf.at[index, at], xf.at[index, at], cs.at[d, h], cr.at[d, h], sib)
 
+    def first_packet(i, buf, send, recv, device):
+        lo, hi = i * step, (i + 1) * step
+        cut = min(max(lo, rows_a), hi)
+        if lo < cut:
+            src = wa_in.at[pl.ds(lo, cut - lo)]
+            remote(src, buf.at[k, pl.ds(lo, cut - lo)], send.at[0, i], recv.at[0, i], device).start()
+        if cut < hi:
+            src = wm_in.at[pl.ds(cut - rows_a, hi - cut)]
+            remote(src, buf.at[k, pl.ds(cut, hi - cut)], send.at[0, i], recv.at[0, i], device).start()
+
     for i in range(CHUNKS):
-        when(k < N - 1, lambda: up(0, i, True).start())
-        when(k > 0, lambda: down(0, i, True).start())
-
-    for load in loads[2:6]:
+        when(k < N - 1, lambda: first_packet(i, ru, us, ur, above))
+        when(k > 0, lambda: first_packet(i, rd, ds, dr, below))
+
+    for load in loads[:4]:
         load.wait()
 
     def scaled(values, exponents, at, size, first):
@@ -127,7 +135,7 @@
     for h in range(PIECES):
         core_copy(0, h).start()
     xf[gz] = xt[...]
-    for load in loads[6:]:
+    for load in loads[4:]:
         load.wait()
 
     def to_core(xj, h):
@@ -255,7 +263,6 @@
     first_sums(1)
     forward(1, 2, "w")
     x_wait(0, 2)
-    pair_sum(k)
     core_wait(0, 2)
     first_sums(2)
     for side in range(2):
@@ -279,7 +286,7 @@
     for n in (2, 3):
         for h in range(PIECES):
             core_wait(n, h)
-    input_sums(1)
+    pair_sum(k)
 
     def gone(s, i):
         when(k < N - 1, lambda: up(s, i).wait_send())
@@ -295,12 +302,13 @@
         next_partial(s + 1, 1)
         gone(s - 3, 1)
         forward(s, 2)
-        input_sums(s - 1)
+        input_sums(s - 2)
         gone(s - 3, 2)
         return carry
 
     lax.fori_loop(3, N - 2, body, 0)
 
+    input_sums(N - 4)
     for s in (N - 2, N - 1):
         for h in range(PIECES):
             for i in range(h * CHUNKS // PIECES, (h + 1) * CHUNKS // PIECES):
@@ -337,8 +345,8 @@
         dxa[...] = total[:rows_a].astype(BF16)
         dxm[...] = total[rows_a:].astype(BF16)
 
-    def last_rows():
-        for i in range(CHUNKS):
+    def last_rows(start, stop):
+        for i in range(start, stop):
             lo, hi = i * step, (i + 1) * step
             for buf, copy, none in ((ru, up, k == 0), (rd, down, k == N - 1)):
                 @pl.when(jnp.logical_not(none))
@@ -352,26 +360,33 @@
             if cut < hi:
                 dwm[cut - rows_a : hi - rows_a] = (p[k, cut:hi] * factor).astype(BF16)
 
-    last_rows()
+    for d in range(NX):
+        for h in range(PIECES):
+            to_core(d, h).wait_send()
+    last_rows(0, 2)
     last_sums()
     for d in (1, 2, 3):
         for h in range(PIECES):
             to_chip((x + d) % NX, h, x).wait_send()
-    for d in range(NX):
-        for h in range(PIECES):
-            to_core(d, h).wait_send()
-    for i in range(CHUNKS):
-        gone(N - 1, i)
+    gone(N - 1, 0)
+    gone(N - 1, 1)
+    last_rows(2, CHUNKS)
+    gone(N - 1, CHUNKS - 1)
 
 
 def write_out(*refs):
-    n = len(refs) // 2
-    sems = refs[-1]
-    copies = [pltpu.make_async_copy(refs[i], refs[n + i], sems.at[i]) for i in range(n)]
-    for copy in copies:
-        copy.start()
-    for copy in copies:
-        copy.wait()
+    n = (len(refs) - 2) // 3
+    results, outputs, staged = refs[:n], refs[n : 2 * n], refs[2 * n : 3 * n]
+    came, went = refs[3 * n :]
+    reads = [pltpu.make_async_copy(results[i], staged[i], came.at[i]) for i in range(n)]
+    writes = [pltpu.make_async_copy(staged[i], outputs[i], went.at[i]) for i in range(n)]
+    for read in reads:
+        read.start()
+    for read, write in zip(reads, writes):
+        read.wait()
+        write.start()
+    for write in writes:
+        write.wait()
 
 
 def on_device(
@@ -434,9 +449,9 @@
     dxa, dxm, dwa, dwm = pl.pallas_call(
         write_out,
         out_shape=shapes,
-        in_specs=[vmem] * 4,
+        in_specs=[hbm] * 4,
         out_specs=[hbm] * 4,
-        scratch_shapes=[dma((4,))],
+        scratch_shapes=[*[pltpu.VMEM(a.shape, a.dtype) for a in shapes], dma((4,)), dma((4,))],
     )(*results)
     return (dxa.T, dxm.T, dwa, dwm)
 

time: 65.7 us -> 64.1 us (0.976)
  Pallas kernels: 64.9 us -> 63.3 us
    pallas_call x1, Pallas kernels: 63 us -> 61.5 us  [on_device(): pl.pallas_call(functools.partial(kernel, factor), out_shape=shapes, in_sp...]
where the time goes in v5:
time: 64.1 us; the launch traced here: 64 us
  Pallas kernels  63.3 us (99%)
    pallas_call x1, Pallas kernels, on_device(): pl.pallas_call(functools.partial(kernel, factor), out_shape=shapes, in_sp...  61.5 us
    pallas_call x1, Pallas kernels, on_device(): pl.pallas_call(write_out, out_shape=shapes, in_specs=[hbm] * 4, out_specs...  1.84 us

profile of v5, /device:TPU:1, one launch (start us, length us, event | category | flops | bytes accessed | tf_op | source)
XLA Modules:
  0.0 64.0 jit_solution(11951866098258368379)
XLA Ops:
  0.6 61.5 %shard_map.111 = (bf16[64,384]{1,0:T(8,128)(2,1)}, bf16[224,384]{1,0:T(8,128)(2,1)}, bf16[64,512]{1,0:T(8,128)(2,1)}, bf16[224,512]{1,0:T(8,128)(2,1)}) custom-call(bf16[64,384]{1,0:T(8,128)(2,1)} %bitcast.7, bf16[224,384]{1,0:T(8,128)(2,1)} %bitcast.6, s32[4,384]{1,0:T(4,128)} %bitcast.9, s32[14,384]{1,0:T(8,128)} %bitcast.8, bf16[384,512]{1,0:T(8,128)(2,1)} %ga_in.1, ...), custom_call_target="tpu_custom_call" | custom-call | tf_op jit(solution)/shard_map/pallas_call | solution.py:425
  62.1 1.8 %shard_map.112 = (bf16[64,384]{1,0:T(8,128)(2,1)}, bf16[224,384]{1,0:T(8,128)(2,1)}, bf16[64,512]{1,0:T(8,128)(2,1)}, bf16[224,512]{1,0:T(8,128)(2,1)}) custom-call(bf16[64,384]{1,0:T(8,128)(2,1)} %get-tuple-element.12.refs_0_, bf16[224,384]{1,0:T(8,128)(2,1)} %get-tuple-element.13.refs_1_, bf16[64,512]{1,0:T(8,128)(2,1)} %get-tuple-element.14.refs_2_, ...), custom_call_target="tpu_custom_call" | custom-call | tf_op jit(solution)/shard_map/pallas_call | solution.py:449

commit v6 on v5

--- a/solution.py
+++ b/solution.py
@@ -36,7 +36,7 @@
     rows = rows_a + rows_m
     step = rows // CHUNKS
     piece = rows // PIECES
-    above, below = (gx, k + 1, gz), (gx, k - 1, gz)
+    above, below = (gx, jnp.minimum(k + 1, N - 1), gz), (gx, jnp.maximum(k - 1, 0), gz)
 
     def chip(other):
         return (gx, k, 2 * other + c)

time: 64.1 us -> 64.1 us (level)
  no operation moved by 1% of the time
where the time goes in v6:
time: 64.1 us; the launch traced here: 64 us
  Pallas kernels  63.3 us (99%)
    pallas_call x1, Pallas kernels, on_device(): pl.pallas_call(functools.partial(kernel, factor), out_shape=shapes, in_sp...  61.5 us
    pallas_call x1, Pallas kernels, on_device(): pl.pallas_call(write_out, out_shape=shapes, in_specs=[hbm] * 4, out_specs...  1.84 us

profile of v6, /device:TPU:1, one launch (start us, length us, event | category | flops | bytes accessed | tf_op | source)
XLA Modules:
  0.0 64.0 jit_solution(12509215439858340057)
XLA Ops:
  0.6 61.5 %shard_map.111 = (bf16[64,384]{1,0:T(8,128)(2,1)}, bf16[224,384]{1,0:T(8,128)(2,1)}, bf16[64,512]{1,0:T(8,128)(2,1)}, bf16[224,512]{1,0:T(8,128)(2,1)}) custom-call(bf16[64,384]{1,0:T(8,128)(2,1)} %bitcast.7, bf16[224,384]{1,0:T(8,128)(2,1)} %bitcast.6, s32[4,384]{1,0:T(4,128)} %bitcast.9, s32[14,384]{1,0:T(8,128)} %bitcast.8, bf16[384,512]{1,0:T(8,128)(2,1)} %ga_in.1, ...), custom_call_target="tpu_custom_call" | custom-call | tf_op jit(solution)/shard_map/pallas_call | solution.py:425
  62.1 1.8 %shard_map.112 = (bf16[64,384]{1,0:T(8,128)(2,1)}, bf16[224,384]{1,0:T(8,128)(2,1)}, bf16[64,512]{1,0:T(8,128)(2,1)}, bf16[224,512]{1,0:T(8,128)(2,1)}) custom-call(bf16[64,384]{1,0:T(8,128)(2,1)} %get-tuple-element.12.refs_0_, bf16[224,384]{1,0:T(8,128)(2,1)} %get-tuple-element.13.refs_1_, bf16[64,512]{1,0:T(8,128)(2,1)} %get-tuple-element.14.refs_2_, ...), custom_call_target="tpu_custom_call" | custom-call | tf_op jit(solution)/shard_map/pallas_call | solution.py:449

commit v7 on v6

--- a/solution.py
+++ b/solution.py
@@ -46,11 +46,11 @@
     def greet(device):
         pl.semaphore_signal(barrier, inc=1, device_id=device, device_id_type=MESH)
 
+    when(k < N - 1, lambda: greet(above))
+    when(k > 0, lambda: greet(below))
     greet(sib)
     for d in (1, 2, 3):
         greet(chip((x + d) % NX))
-    when(k < N - 1, lambda: greet(above))
-    when(k > 0, lambda: greet(below))
 
     loads = [
         pltpu.make_async_copy(src, dst, ins.at[i])
@@ -253,15 +253,15 @@
 
     grad_dot(w, k)
     forward(1, 0, "w")
+    forward(1, 1, "w")
     x_wait(0, 0)
     when(held, x_start)
     core_wait(0, 0)
     first_sums(0)
-    forward(1, 1, "w")
+    forward(1, 2, "w")
     x_wait(0, 1)
     core_wait(0, 1)
     first_sums(1)
-    forward(1, 2, "w")
     x_wait(0, 2)
     core_wait(0, 2)
     first_sums(2)
@@ -271,10 +271,10 @@
     forward(2, 0)
     for h in range(PIECES):
         x_wait(1, h)
+    input_part(1, 0)
+    forward(2, 1)
     for h in range(PIECES):
         core_wait(1, h)
-    input_part(1, 0)
-    forward(2, 1)
     for h in range(PIECES):
         x_wait(2, h)
     input_part(1, 1)

time: 64.1 us -> 64.1 us (level)
  no operation moved by 1% of the time
where the time goes in v7:
time: 64.1 us; the launch traced here: 63.9 us
  Pallas kernels  63.3 us (99%)
    pallas_call x1, Pallas kernels, on_device(): pl.pallas_call(functools.partial(kernel, factor), out_shape=shapes, in_sp...  61.5 us
    pallas_call x1, Pallas kernels, on_device(): pl.pallas_call(write_out, out_shape=shapes, in_specs=[hbm] * 4, out_specs...  1.84 us

profile of v7, /device:TPU:1, one launch (start us, length us, event | category | flops | bytes accessed | tf_op | source)
XLA Modules:
  0.0 63.9 jit_solution(3875323931638861861)
XLA Ops:
  0.6 61.5 %shard_map.111 = (bf16[64,384]{1,0:T(8,128)(2,1)}, bf16[224,384]{1,0:T(8,128)(2,1)}, bf16[64,512]{1,0:T(8,128)(2,1)}, bf16[224,512]{1,0:T(8,128)(2,1)}) custom-call(bf16[64,384]{1,0:T(8,128)(2,1)} %bitcast.7, bf16[224,384]{1,0:T(8,128)(2,1)} %bitcast.6, s32[4,384]{1,0:T(4,128)} %bitcast.9, s32[14,384]{1,0:T(8,128)} %bitcast.8, bf16[384,512]{1,0:T(8,128)(2,1)} %ga_in.1, ...), custom_call_target="tpu_custom_call" | custom-call | tf_op jit(solution)/shard_map/pallas_call | solution.py:425
  62.1 1.8 %shard_map.112 = (bf16[64,384]{1,0:T(8,128)(2,1)}, bf16[224,384]{1,0:T(8,128)(2,1)}, bf16[64,512]{1,0:T(8,128)(2,1)}, bf16[224,512]{1,0:T(8,128)(2,1)}) custom-call(bf16[64,384]{1,0:T(8,128)(2,1)} %get-tuple-element.12.refs_0_, bf16[224,384]{1,0:T(8,128)(2,1)} %get-tuple-element.13.refs_1_, bf16[64,512]{1,0:T(8,128)(2,1)} %get-tuple-element.14.refs_2_, ...), custom_call_target="tpu_custom_call" | custom-call | tf_op jit(solution)/shard_map/pallas_call | solution.py:449

commit v8 on v6

--- a/solution.py
+++ b/solution.py
@@ -25,9 +25,10 @@
 
 
 def kernel(
-    factor, xa_in, xm_in, ea_in, em_in, ga_in, gm_in, wa_in, wm_in, dxa, dxm, dwa, dwm,
+    factor, xa_in, xm_in, ea_in, em_in, ga_in, gm_in, wa_in, wm_in, dxa_out, dxm_out, dwa_out, dwm_out,
+    dxa, dxm, dwa, dwm,
     xa, xm, ea, em, ga, gm, w, xt, xf, ru, rd, p, qk, qs, qc, qp, qr, total,
-    ins, us, ur, ds, dr, xs, xr, cs, cr, qcs, qcr, qxs, qxr,
+    ins, outs, us, ur, ds, dr, xs, xr, cs, cr, qcs, qcr, qxs, qxr,
 ):
     gx, k, gz = lax.axis_index("gx"), lax.axis_index("gy"), lax.axis_index("gz")
     x, c = gz // 2, gz % 2
@@ -336,6 +337,9 @@
         for i in range(CHUNKS):
             gone(s, i)
 
+    def results(src, dst, i):
+        return pltpu.make_async_copy(src, dst, outs.at[i])
+
     def last_sums():
         for d in (1, 3, 2):
             other = (x - d + NX) % NX
@@ -344,6 +348,8 @@
             total[...] = total[...] + qr[other].astype(F32)
         dxa[...] = total[:rows_a].astype(BF16)
         dxm[...] = total[rows_a:].astype(BF16)
+        results(dxa, dxa_out, 0).start()
+        results(dxm, dxm_out, 1).start()
 
     def last_rows(start, stop):
         for i in range(start, stop):
@@ -359,6 +365,20 @@
                 dwa[lo:cut] = (p[k, lo:cut] * factor).astype(BF16)
             if cut < hi:
                 dwm[cut - rows_a : hi - rows_a] = (p[k, cut:hi] * factor).astype(BF16)
+            for copy in row_copies(i):
+                copy.start()
+
+    def row_copies(i):
+        lo, hi = i * step, (i + 1) * step
+        cut = min(max(lo, rows_a), hi)
+        copies = []
+        if lo < cut:
+            at = pl.ds(lo, cut - lo)
+            copies.append(results(dwa.at[at], dwa_out.at[at], 2))
+        if cut < hi:
+            at = pl.ds(cut - rows_a, hi - cut)
+            copies.append(results(dwm.at[at], dwm_out.at[at], 3 + i))
+        return copies
 
     for d in range(NX):
         for h in range(PIECES):
@@ -372,6 +392,11 @@
     gone(N - 1, 1)
     last_rows(2, CHUNKS)
     gone(N - 1, CHUNKS - 1)
+    results(dxa, dxa_out, 0).wait()
+    results(dxm, dxm_out, 1).wait()
+    for i in range(CHUNKS):
+        for copy in row_copies(i):
+            copy.wait()
 
 
 def write_out(*refs):
@@ -426,8 +451,9 @@
         functools.partial(kernel, factor),
         out_shape=shapes,
         in_specs=[hbm] * 8,
-        out_specs=[vmem] * 4,
+        out_specs=[hbm] * 4,
         scratch_shapes=[
+            *[pltpu.VMEM(a.shape, a.dtype) for a in shapes],
             *[pltpu.VMEM(a.shape, a.dtype) for a in inputs[:6]],
             pltpu.VMEM((rows, width), BF16),
             pltpu.VMEM((rows, tokens), BF16),
@@ -439,6 +465,7 @@
             *[pltpu.VMEM((NX, rows, tokens), BF16)] * 4,
             pltpu.VMEM((rows, tokens), F32),
             dma((8,)),
+            dma((3 + CHUNKS,)),
             *[dma((N, CHUNKS))] * 4,
             *[dma((NX, PIECES))] * 8,
         ],

time: 64.1 us -> 63.8 us (level)
  Pallas kernels: 63.3 us -> 62.6 us
    pallas_call x1, Pallas kernels: 61.5 us -> 60.8 us  [on_device(): pl.pallas_call(functools.partial(kernel, factor), out_shape=shapes, in_sp...]
where the time goes in v8:
time: 63.8 us; the launch traced here: 63.3 us
  Pallas kernels  62.6 us (98%)
  between operations  0.64 us (1%)
    pallas_call x1, Pallas kernels, on_device(): pl.pallas_call(functools.partial(kernel, factor), out_shape=shapes, in_sp...  60.8 us
    pallas_call x1, Pallas kernels, on_device(): pl.pallas_call(write_out, out_shape=shapes, in_specs=[hbm] * 4, out_specs...  1.84 us

profile of v8, /device:TPU:1, one launch (start us, length us, event | category | flops | bytes accessed | tf_op | source)
XLA Modules:
  0.0 63.3 jit_solution(2866072603195269881)
XLA Ops:
  0.6 60.8 %shard_map.111 = (bf16[64,384]{1,0:T(8,128)(2,1)}, bf16[224,384]{1,0:T(8,128)(2,1)}, bf16[64,512]{1,0:T(8,128)(2,1)}, bf16[224,512]{1,0:T(8,128)(2,1)}) custom-call(bf16[64,384]{1,0:T(8,128)(2,1)} %bitcast.7, bf16[224,384]{1,0:T(8,128)(2,1)} %bitcast.6, s32[4,384]{1,0:T(4,128)} %bitcast.9, s32[14,384]{1,0:T(8,128)} %bitcast.8, bf16[384,512]{1,0:T(8,128)(2,1)} %ga_in.1, ...), custom_call_target="tpu_custom_call" | custom-call | tf_op jit(solution)/shard_map/pallas_call | solution.py:450
  61.4 1.8 %shard_map.112 = (bf16[64,384]{1,0:T(8,128)(2,1)}, bf16[224,384]{1,0:T(8,128)(2,1)}, bf16[64,512]{1,0:T(8,128)(2,1)}, bf16[224,512]{1,0:T(8,128)(2,1)}) custom-call(bf16[64,384]{1,0:T(8,128)(2,1)} %get-tuple-element.12.refs_0_, bf16[224,384]{1,0:T(8,128)(2,1)} %get-tuple-element.13.refs_1_, bf16[64,512]{1,0:T(8,128)(2,1)} %get-tuple-element.14.refs_2_, ...), custom_call_target="tpu_custom_call" | custom-call | tf_op jit(solution)/shard_map/pallas_call | solution.py:476
